TPU v7x, 32 devices: a whole 2x2x4 slice. The times are simulated.
32 devices in a mesh: ep: 8 (over y, x, core), ex: 4 (over z).
Axes of the slice: x: 2, y: 2, z: 4, core: 2. Of those that a mesh axis runs over, the one named last changes fastest.
Arguments:
- dout: bfloat16 [1024, 7168], P(('ep', 'ex')), may hold values from -1.5 to 1.5
- gates: bfloat16 [1024, 8], P(('ep', 'ex')), may hold values from 0.049804688 to 0.59765625
- saved_down_input: bfloat16 [1024, 8, 1024], P(('ep', 'ex')), may hold values from -3 to 3
- routing: int32 [1024, 8], P(('ep', 'ex')), may hold values from 0 to 27, as said below
- placement: int32 [32], replicated, may hold values from 0 to 27, as said below
- partner: int32 [32], replicated, may hold values from 0 to 31, as said below
- frozen: bfloat16 [32, 1024, 7168], P(('ep', 'ex')), as said below
- colscale: float32 [32, 7168], P(('ep', 'ex')), may hold values from 0.5 to 2, as said below
- adapter_down_factor: bfloat16 [32, 1024, 64], P(('ep', 'ex')), as said below
- adapter_up_factor: bfloat16 [32, 64, 7168], P(('ep', 'ex')), as said below
- first_moment_down: bfloat16 [32, 1024, 64], P(('ep', 'ex')), as said below
- second_moment_down: bfloat16 [32, 1024, 64], P(('ep', 'ex')), may hold values from 0.1 to 4, as said below
- first_moment_up: bfloat16 [32, 64, 7168], P(('ep', 'ex')), as said below
- second_moment_up: bfloat16 [32, 64, 7168], P(('ep', 'ex')), may hold values from 0.1 to 4, as said below
Outputs:
- routed_input_gradient: bfloat16 [1024, 8, 1024], P(('ep', 'ex'))
- combine_gate_gradient: bfloat16 [1024, 8], P(('ep', 'ex'))
- updated_down_factor: bfloat16 [32, 1024, 64], P(('ep', 'ex'))
- updated_up_factor: bfloat16 [32, 64, 7168], P(('ep', 'ex'))
- updated_first_moment_down: bfloat16 [32, 1024, 64], P(('ep', 'ex'))
- updated_second_moment_down: bfloat16 [32, 1024, 64], P(('ep', 'ex'))
- updated_first_moment_up: bfloat16 [32, 64, 7168], P(('ep', 'ex'))
- updated_second_moment_up: bfloat16 [32, 64, 7168], P(('ep', 'ex'))
Inputs may be any that keep to these rules, and one draw needn't show every extreme that they name: `routing`: each token names 8 different experts. Of each device's tokens, an expert with two slots is named by exactly 16, every other expert by exactly 8. `placement`: every expert is held by one slot, or by two slots of one expert group (equal index along ep); 4 experts hold two slots, each in a group of its own. placement[partner[s]] = placement[s]; partner[s] is the other slot of the same expert, or s if the expert holds one slot. `frozen`: slots of the same expert hold equal values. `colscale`: slots of the same expert hold equal values. `adapter_down_factor`: slots of the same expert hold equal values. `adapter_up_factor`: slots of the same expert hold equal values. `first_moment_down`: slots of the same expert hold equal values. `second_moment_down`: slots of the same expert hold equal values. `first_moment_up`: slots of the same expert hold equal values. `second_moment_up`: slots of the same expert hold equal values.
All inputs are finite; a program needn't handle non-finite values.
Results may differ from a plain program's by a relative error of at most 0.005.
Values may be sent and summed in bfloat16 or wider, within the bound.
No kernel may reach another device: no remote copies, remote signals or barrier semaphores. Data moves between devices by JAX's collectives and lax.ppermute only.
A program may use at most 128 MiB of HBM per device.

v0:
```python
import jax
import jax.numpy as jnp
from jax import lax
from jax.sharding import PartitionSpec as P

adapter_scale = 2.0
beta_one = 0.9
beta_two = 0.999
adam_eps = 1e-08
learn_rate = 0.01
weight_decay = 0.01
adam_step = 10


def expert_row_block(
    hidden_row_block,
    output_gradient_rows,
    gate_row_values,
    frozen_w,
    scale,
    adapter_down_projected,
    low_b,
):
    gate_broadcast_wide = gate_row_values.astype(jnp.float32)[:, None]
    dout_wide = output_gradient_rows.astype(jnp.float32)
    adapter_output_gradient = (gate_broadcast_wide * dout_wide).astype(jnp.bfloat16)
    dsc_low = (dout_wide * scale[None, :]).astype(jnp.bfloat16)
    backward_through_adapter = jnp.dot(
        adapter_output_gradient, low_b.T, preferred_element_type=jnp.float32
    ).astype(jnp.bfloat16)
    backward_through_frozen = jnp.dot(dsc_low, frozen_w.T, preferred_element_type=jnp.float32)
    incoming_input_gradient = (
        gate_broadcast_wide * backward_through_frozen
        + adapter_scale
        * jnp.dot(
            backward_through_adapter, adapter_down_projected.T, preferred_element_type=jnp.float32
        )
    )
    adapter_down_product = jnp.dot(
        hidden_row_block, adapter_down_projected, preferred_element_type=jnp.float32
    ).astype(jnp.bfloat16)
    output_gradient_adapter = jnp.dot(
        output_gradient_rows, low_b.T, preferred_element_type=jnp.float32
    )
    gated_output = jnp.sum(
        hidden_row_block.astype(jnp.float32) * backward_through_frozen, axis=1
    ) + adapter_scale * jnp.sum(
        adapter_down_product.astype(jnp.float32) * output_gradient_adapter, axis=1
    )
    down_factor_gradient = adapter_scale * jnp.dot(
        hidden_row_block.T, backward_through_adapter, preferred_element_type=jnp.float32
    )
    up_factor_gradient = adapter_scale * jnp.dot(
        adapter_down_product.T, adapter_output_gradient, preferred_element_type=jnp.float32
    )
    return (
        incoming_input_gradient.astype(jnp.bfloat16),
        gated_output.astype(jnp.bfloat16),
        down_factor_gradient,
        up_factor_gradient,
    )


def apply_adam_update(weights, moment, second_moment, gradient):
    weights_wide = weights.astype(jnp.float32)
    first = beta_one * moment.astype(jnp.float32) + (1.0 - beta_one) * gradient
    second = beta_two * second_moment.astype(jnp.float32) + (1.0 - beta_two) * gradient * gradient
    first_hat = first / (1.0 - beta_one**adam_step)
    second_hat = second / (1.0 - beta_two**adam_step)
    fresh = weights_wide - learn_rate * (
        first_hat / (jnp.sqrt(second_hat) + adam_eps) + weight_decay * weights_wide
    )
    return (fresh.astype(jnp.bfloat16), first.astype(jnp.bfloat16), second.astype(jnp.bfloat16))


def per_device(
    dout,
    gates,
    saved_down_input,
    routing,
    placement,
    partner,
    frozen,
    colscale,
    adapter_down_factor,
    adapter_up_factor,
    first_moment_down,
    second_moment_down,
    first_moment_up,
    second_moment_up,
):
    groups = lax.axis_size("ep")
    members = lax.axis_size("ex")
    slot_count = groups * members
    tok_rows, top_count = routing.shape
    model_width = dout.shape[1]
    hidden = saved_down_input.shape[2]
    adapter_rank_width = adapter_down_factor.shape[2]
    row_count = tok_rows * top_count
    capacity = row_count // slot_count
    expert_flat = routing.reshape(row_count)
    slot_ids = jnp.arange(slot_count, dtype=jnp.int32)
    holds_expert = placement[None, :] == expert_flat[:, None]
    first_slot = jnp.min(jnp.where(holds_expert, slot_ids[None, :], slot_count), axis=1)
    last_slot = jnp.max(jnp.where(holds_expert, slot_ids[None, :], -1), axis=1)
    row_ids = jnp.arange(row_count, dtype=jnp.int32)
    earlier = row_ids[None, :] < row_ids[:, None]
    same_expert = expert_flat[None, :] == expert_flat[:, None]
    turn_index = jnp.sum((same_expert & earlier).astype(jnp.int32), axis=1)
    target = jnp.where(turn_index % 2 == 1, last_slot, first_slot)
    same_slot = target[None, :] == target[:, None]
    position = jnp.sum((same_slot & earlier).astype(jnp.int32), axis=1)
    buffer_row = target * capacity + position
    row_width = model_width + hidden
    row_data = jnp.concatenate(
        [jnp.broadcast_to(dout[:, None, :], (tok_rows, top_count, model_width)), saved_down_input],
        axis=2,
    ).reshape(row_count, row_width)
    outgoing = (
        jnp.zeros((slot_count * capacity, row_width), jnp.bfloat16).at[buffer_row].set(row_data)
    )
    outgoing_gate = (
        jnp.zeros((slot_count * capacity,), jnp.bfloat16)
        .at[buffer_row]
        .set(gates.reshape(row_count))
    )
    incoming, incoming_gate = (
        lax.all_to_all(
            outgoing.reshape(slot_count, capacity, row_width),
            ("ep", "ex"),
            split_axis=0,
            concat_axis=0,
            tiled=True,
        ),
        lax.all_to_all(
            outgoing_gate.reshape(slot_count, capacity),
            ("ep", "ex"),
            split_axis=0,
            concat_axis=0,
            tiled=True,
        ),
    )
    live_rows = slot_count * capacity
    incoming = incoming.reshape(live_rows, row_width)
    output_gradient_rows = incoming[:, :model_width]
    hidden_row_block = incoming[:, model_width:]
    incoming_input_gradient, gated_output, down_factor_gradient, up_factor_gradient = (
        expert_row_block(
            hidden_row_block,
            output_gradient_rows,
            incoming_gate.reshape(live_rows),
            frozen[0],
            colscale[0],
            adapter_down_factor[0],
            adapter_up_factor[0],
        )
    )
    returned_grad, returned_gate = (
        lax.all_to_all(
            incoming_input_gradient.reshape(slot_count, capacity, hidden),
            ("ep", "ex"),
            split_axis=0,
            concat_axis=0,
            tiled=True,
        ),
        lax.all_to_all(
            gated_output.reshape(slot_count, capacity),
            ("ep", "ex"),
            split_axis=0,
            concat_axis=0,
            tiled=True,
        ),
    )
    routed_input_gradient = returned_grad.reshape(live_rows, hidden)[buffer_row].reshape(
        tok_rows, top_count, hidden
    )
    combine_gate_gradient = returned_gate.reshape(live_rows)[buffer_row].reshape(
        tok_rows, top_count
    )
    own_member = lax.axis_index("ex")
    own_slot = lax.axis_index("ep") * members + own_member
    mate_slot = jnp.sum(jnp.where(slot_ids == own_slot, partner, 0))
    mate_member = mate_slot % members
    flat_a = down_factor_gradient.reshape(1, hidden * adapter_rank_width // 128, 128)
    flat_b = up_factor_gradient.reshape(1, adapter_rank_width, model_width)
    pieces = (
        lax.all_gather(flat_a.astype(jnp.bfloat16), "ex", axis=0, tiled=True).astype(jnp.float32),
        lax.all_gather(flat_b.astype(jnp.bfloat16), "ex", axis=0, tiled=True).astype(jnp.float32),
    )
    length = pieces[0].shape[0]
    members_here = jnp.arange(length, dtype=jnp.int32)
    chosen = ((members_here == own_member) | (members_here == mate_member)).astype(jnp.float32)
    summed_down_gradient = jnp.zeros(flat_a.shape[1:], jnp.float32) + jnp.sum(
        chosen[:, None, None] * pieces[0], axis=0
    )
    summed_up_gradient = jnp.zeros(flat_b.shape[1:], jnp.float32) + jnp.sum(
        chosen[:, None, None] * pieces[1], axis=0
    )
    summed_down_gradient = summed_down_gradient.reshape(1, hidden, adapter_rank_width)
    summed_up_gradient = summed_up_gradient.reshape(1, adapter_rank_width, model_width)
    updated_down_factor, updated_first_moment_down, updated_second_moment_down = apply_adam_update(
        adapter_down_factor, first_moment_down, second_moment_down, summed_down_gradient
    )
    updated_up_factor, updated_first_moment_up, updated_second_moment_up = apply_adam_update(
        adapter_up_factor, first_moment_up, second_moment_up, summed_up_gradient
    )
    return (
        routed_input_gradient,
        combine_gate_gradient,
        updated_down_factor,
        updated_up_factor,
        updated_first_moment_down,
        updated_second_moment_down,
        updated_first_moment_up,
        updated_second_moment_up,
    )


def solution(mesh):
    placed = (
        P(("ep", "ex"), None),
        P(("ep", "ex"), None),
        P(("ep", "ex"), None, None),
        P(("ep", "ex"), None),
        P(),
        P(),
        P(("ep", "ex"), None, None),
        P(("ep", "ex"), None),
        P(("ep", "ex"), None, None),
        P(("ep", "ex"), None, None),
        P(("ep", "ex"), None, None),
        P(("ep", "ex"), None, None),
        P(("ep", "ex"), None, None),
        P(("ep", "ex"), None, None),
    )
    return jax.shard_map(
        per_device,
        mesh=mesh,
        in_specs=placed,
        out_specs=(
            P(("ep", "ex"), None, None),
            P(("ep", "ex"), None),
            P(("ep", "ex"), None, None),
            P(("ep", "ex"), None, None),
            P(("ep", "ex"), None, None),
            P(("ep", "ex"), None, None),
            P(("ep", "ex"), None, None),
            P(("ep", "ex"), None, None),
        ),
        check_vma=False,
    )
```

profile of v0, /device:TPU:0, one launch (start us, length us, event | category | flops | bytes accessed | tf_op | source)
XLA Modules:
  0.0 243.8 jit_solution(11940484604645975405)
XLA Ops:
  7.2 0.8 copy.56
  8.3 0.8 fusion.49
  9.2 0.8 copy.57
  10.1 2.2 scatter_custom_fusion
  12.3 0.7 all_to_all.21
  13.0 7.3 %all-to-all-start = ((bf16[32,1,8]{2,1,0:T(2,128)(2,1)}), bf16[32,1,8]{2,1,0:T(2,128)(2,1)S(1)}, u32[]{:S(2)}, u32[]{:S(2)}) async-start(bf16[32,1,8]{2,1,0:T(2,128)(2,1)} %all_to_all.21), calls=%async_computation | async-start | bytes 32768 | tf_op jit(solution)/shard_map/all_to_all | solution.py:135
  20.3 3.3 %broadcast_in_dim.56 = bf16[32,8,7168]{2,1,0:T(8,128)(2,1)} broadcast(bf16[32,7168]{1,0:T(8,128)(2,1)} %param.14), dimensions={0,2} | broadcast | bytes 4128768 | tf_op jit(solution)/shard_map/broadcast_in_dim | solution.py:116
  23.6 10.0 %scatter_custom_fusion.1 = bf16[256,8192]{1,0:T(8,128)(2,1)} fusion(s32[256]{0:T(256)S(1)} %bitcast.56, bf16[32,8,1024]{2,1,0:T(8,128)(2,1)S(1)} %copy-done.3, bf16[]{:T(256)} %constant.102, bf16[32,8,7168]{2,1,0:T(8,128)(2,1)} %broadcast_in_dim.56, bf16[]{:T(256)} %constant.25.clone.1), kind=kCustom, calls=%fused_computation.15 | custom fusion | flops 8388608 | bytes 8388612 | tf_op jit(solution)/shard_map/scatter | solution.py:120
  33.6 6.0 %all-to-all-start.1 = ((bf16[32,8,8192]{2,1,0:T(8,128)(2,1)}), bf16[32,8,8192]{2,1,0:T(8,128)(2,1)}, u32[]{:S(2)}, u32[]{:S(2)}) async-start(bf16[32,8,8192]{2,1,0:T(8,128)(2,1)} %bitcast.49), calls=%async_computation.1 | async-start | bytes 8388608 | tf_op jit(solution)/shard_map/all_to_all | solution.py:128
  39.6 0.2 all-gather.3.cloned.1.call-start
  39.9 91.9 %all-to-all-done.1 = bf16[32,8,8192]{2,1,0:T(8,128)(2,1)} async-done(((bf16[32,8,8192]{2,1,0:T(8,128)(2,1)}), bf16[32,8,8192]{2,1,0:T(8,128)(2,1)}, u32[]{:S(2)}, u32[]{:S(2)}) %all-to-all-start.1) | async-done | bytes 4194336 | tf_op jit(solution)/shard_map/all_to_all | solution.py:128
  131.8 1.3 convolution_convert_fusion
  133.2 4.1 %fusion.2 = bf16[64,7168]{1,0:T(8,128)(2,1)} fusion(bf16[256,64]{0,1:T(8,128)(2,1)S(1)} %convolution_convert_fusion, f32[256]{0:T(256)S(1)} %reshape.282, bf16[256,8192]{1,0:T(8,128)(2,1)} %bitcast.7), kind=kOutput, calls=%fused_computation.9 | convolution fusion | flops 241303552 | bytes 4621312 | tf_op jit(solution)/shard_map/dot_general | solution.py:53
  137.3 0.6 fusion.52
  139.9 3.3 %fusion.27 = f32[256]{0:T(256)S(1)} fusion(bf16[256,8192]{1,0:T(8,128)(2,1)} %bitcast.7, bf16[1,64,7168]{2,1,0:T(8,128)(2,1)S(1)} %copy-done, bf16[256,64]{0,1:T(8,128)(2,1)S(1)} %convolution_convert_fusion), kind=kOutput, calls=%fused_computation.41 | convolution fusion | flops 234929920 | bytes 4621312 | tf_op jit(solution)/shard_map/dot_general | solution.py:42
  143.2 11.3 %multiply_reduce_fusion.1 = (f32[256]{0:T(256)S(1)}, f32[256,1024]{1,0:T(8,128)S(1)}) fusion(bf16[256,8192]{1,0:T(8,128)(2,1)} %bitcast.7, bf16[1,1024,7168]{2,1,0:T(8,128)(2,1)} %param.20, f32[7168]{0:T(1024)S(1)} %bitcast.59), kind=kOutput, calls=%fused_computation.44 | convolution fusion | flops 3764387584 | bytes 19952640 | tf_op jit(solution)/shard_map/dot_general | solution.py:31
  154.4 0.7 convert_element_type.158
  155.1 5.4 %all-to-all-start.3 = ((bf16[32,1,8]{2,1,0:T(2,128)(2,1)}), bf16[32,1,8]{2,1,0:T(2,128)(2,1)S(1)}, u32[]{:S(2)}, u32[]{:S(2)}) async-start(bf16[32,1,8]{2,1,0:T(2,128)(2,1)} %convert_element_type.158), calls=%async_computation.3 | async-start | bytes 32768 | tf_op jit(solution)/shard_map/all_to_all | solution.py:166
  160.5 3.3 %convolution_convert_fusion.1 = bf16[256,64]{0,1:T(8,128)(2,1)S(1)} fusion(f32[256]{0:T(256)S(1)} %reshape.282, bf16[256,8192]{1,0:T(8,128)(2,1)} %bitcast.7, bf16[1,64,7168]{2,1,0:T(8,128)(2,1)S(1)} %copy-done), kind=kOutput, calls=%fused_computation.40 | convolution fusion | flops 240402432 | bytes 4621312 | tf_op jit(solution)/shard_map/dot_general | solution.py:28
  163.9 1.1 fusion.22
  165.0 2.9 %all-to-all-done.3 = bf16[32,1,8]{2,1,0:T(2,128)(2,1)S(1)} async-done(((bf16[32,1,8]{2,1,0:T(2,128)(2,1)}), bf16[32,1,8]{2,1,0:T(2,128)(2,1)S(1)}, u32[]{:S(2)}, u32[]{:S(2)}) %all-to-all-start.3) | async-done | bytes 544 | tf_op jit(solution)/shard_map/all_to_all | solution.py:166
  167.9 3.0 %all-to-all-start.2 = ((bf16[32,8,1024]{2,1,0:T(8,128)(2,1)}), bf16[32,8,1024]{2,1,0:T(8,128)(2,1)S(1)}, u32[]{:S(2)}, u32[]{:S(2)}) async-start(bf16[32,8,1024]{2,1,0:T(8,128)(2,1)} %fusion.22), calls=%async_computation.2 | async-start | bytes 1048576 | tf_op jit(solution)/shard_map/all_to_all | solution.py:159
  170.9 1.3 fusion.23
  172.5 41.9 %all_gather.6 = bf16[4,512,128]{2,1,0:T(8,128)(2,1)S(1)} all-gather(bf16[1,512,128]{2,1,0:T(8,128)(2,1)S(1)} %convert_element_type.141), channel_id=1, replica_groups=mesh['ep'=8,'ex'=4] {'ex'}, dimensions={0}, use_global_device_ids=true | all-gather | bytes 655360 | tf_op jit(solution)/shard_map/all_gather | solution.py:187
  214.4 0.2 multiply_reduce_fusion
  214.9 1.0 fusion.45
  216.1 1.9 gather_fusion.1
  218.1 0.7 copy.64
  218.8 2.0 gather_fusion
  220.7 9.4 %all-gather.3.cloned.1.call-done = bf16[256,7168]{1,0:T(8,128)(2,1)} async-done(((bf16[64,7168]{1,0:T(8,128)(2,1)}), bf16[256,7168]{1,0:T(8,128)(2,1)}) %all-gather.3.cloned.1.call-update) | async-done | bytes 3670032 | tf_op jit(solution)/shard_map/all_gather | solution.py:188
  230.2 3.1 %fusion.5 = f32[64,7168]{1,0:T(8,128)S(1)} fusion(bf16[4,64,7168]{2,1,0:T(8,128)(2,1)} %bitcast.50, f32[4]{0:T(128)S(1)} %or_convert_fusion), kind=kLoop, calls=%fused_computation.13 | loop fusion | flops 5046272 | bytes 5505040 | tf_op jit(solution)/shard_map/reduce_sum | solution.py:196
  233.3 3.7 %fusion.33 = (bf16[1,64,7168]{2,1,0:T(8,128)(2,1)}, bf16[1,64,7168]{2,1,0:T(8,128)(2,1)}, bf16[1,64,7168]{2,1,0:T(8,128)(2,1)}) fusion(f32[64,7168]{1,0:T(8,128)S(1)} %fusion.5, bf16[1,64,7168]{2,1,0:T(8,128)(2,1)S(1)} %copy-done.1, bf16[1,64,7168]{2,1,0:T(8,128)(2,1)S(1)} %copy-done.2, bf16[1,64,7168]{2,1,0:T(8,128)(2,1)S(1)} %copy-done), kind=kLoop, calls=%fused_computation.45 | loop fusion | flops 9633792 | bytes 7340032 | tf_op jit(solution)/shard_map/convert_element_type | solution.py:73
  (39 shorter events, 1.7 us)
Async XLA Ops:
  7.2 16.5 %copy-start.3 = (bf16[32,8,1024]{2,1,0:T(8,128)(2,1)S(1)}, bf16[32,8,1024]{2,1,0:T(8,128)(2,1)}, u32[]{:S(2)}) copy-start(bf16[32,8,1024]{2,1,0:T(8,128)(2,1)} %param.16) | copy-start | bytes 1572868
  13.0 20.6 %all-to-all-start = ((bf16[32,1,8]{2,1,0:T(2,128)(2,1)}), bf16[32,1,8]{2,1,0:T(2,128)(2,1)S(1)}, u32[]{:S(2)}, u32[]{:S(2)}) async-start(bf16[32,1,8]{2,1,0:T(2,128)(2,1)} %all_to_all.21), calls=%async_computation | async-start | bytes 32768 | tf_op jit(solution)/shard_map/all_to_all | solution.py:135
  33.6 98.2 %copy-start.4 = (bf16[1,1024,64]{1,2,0:T(8,128)(2,1)S(1)}, bf16[1,1024,64]{1,2,0:T(8,128)(2,1)}, u32[]{:S(2)}) copy-start(bf16[1,1024,64]{1,2,0:T(8,128)(2,1)} %param.22) | copy-start | bytes 393220
  33.6 98.2 %all-to-all-start.1 = ((bf16[32,8,8192]{2,1,0:T(8,128)(2,1)}), bf16[32,8,8192]{2,1,0:T(8,128)(2,1)}, u32[]{:S(2)}, u32[]{:S(2)}) async-start(bf16[32,8,8192]{2,1,0:T(8,128)(2,1)} %bitcast.49), calls=%async_computation.1 | async-start | bytes 8388608 | tf_op jit(solution)/shard_map/all_to_all | solution.py:128
  39.6 190.6 %all-gather.3.cloned.1.call-start = ((), (), s32[]{:S(2)}) async-start(), calls=%async_computation.4 | async-start | bytes 4587520 | tf_op jit(solution)/shard_map/all_gather | solution.py:188
  133.1 4.1 %copy-start.8 = (s32[32]{0:T(128)S(1)}, s32[32]{0:T(128)}, u32[]{:S(2)}) copy-start(s32[32]{0:T(128)} %param.19) | copy-start | bytes 388
  133.1 6.7 %copy-start = (bf16[1,64,7168]{2,1,0:T(8,128)(2,1)S(1)}, bf16[1,64,7168]{2,1,0:T(8,128)(2,1)}, u32[]{:S(2)}) copy-start(bf16[1,64,7168]{2,1,0:T(8,128)(2,1)} %param.23) | copy-start | bytes 2752516
  137.2 5.9 %copy-start.7 = (f32[1,7168]{1,0:T(1,128)S(1)}, f32[1,7168]{1,0:T(1,128)}, u32[]{:S(2)}) copy-start(f32[1,7168]{1,0:T(1,128)} %param.21) | copy-start | bytes 86020
  155.1 12.7 %all-to-all-start.3 = ((bf16[32,1,8]{2,1,0:T(2,128)(2,1)}), bf16[32,1,8]{2,1,0:T(2,128)(2,1)S(1)}, u32[]{:S(2)}, u32[]{:S(2)}) async-start(bf16[32,1,8]{2,1,0:T(2,128)(2,1)} %convert_element_type.158), calls=%async_computation.3 | async-start | bytes 32768 | tf_op jit(solution)/shard_map/all_to_all | solution.py:166
  163.9 51.0 %copy-start.5 = (bf16[1,1024,64]{1,2,0:T(8,128)(2,1)S(1)}, bf16[1,1024,64]{1,2,0:T(8,128)(2,1)}, u32[]{:S(2)}) copy-start(bf16[1,1024,64]{1,2,0:T(8,128)(2,1)} %param.25) | copy-start | bytes 393220
  163.9 51.0 %copy-start.6 = (bf16[1,1024,64]{1,2,0:T(8,128)(2,1)S(1)}, bf16[1,1024,64]{1,2,0:T(8,128)(2,1)}, u32[]{:S(2)}) copy-start(bf16[1,1024,64]{1,2,0:T(8,128)(2,1)} %param.24) | copy-start | bytes 393220
  167.9 50.9 %all-to-all-start.2 = ((bf16[32,8,1024]{2,1,0:T(8,128)(2,1)}), bf16[32,8,1024]{2,1,0:T(8,128)(2,1)S(1)}, u32[]{:S(2)}, u32[]{:S(2)}) async-start(bf16[32,8,1024]{2,1,0:T(8,128)(2,1)} %fusion.22), calls=%async_computation.2 | async-start | bytes 1048576 | tf_op jit(solution)/shard_map/all_to_all | solution.py:159
  220.7 12.5 %copy-start.1 = (bf16[1,64,7168]{2,1,0:T(8,128)(2,1)S(1)}, bf16[1,64,7168]{2,1,0:T(8,128)(2,1)}, u32[]{:S(2)}) copy-start(bf16[1,64,7168]{2,1,0:T(8,128)(2,1)} %param.27) | copy-start | bytes 2752516
  220.7 12.5 %copy-start.2 = (bf16[1,64,7168]{2,1,0:T(8,128)(2,1)S(1)}, bf16[1,64,7168]{2,1,0:T(8,128)(2,1)}, u32[]{:S(2)}) copy-start(bf16[1,64,7168]{2,1,0:T(8,128)(2,1)} %param.26) | copy-start | bytes 2752516
Sparse Core Ops, SparseCore 0:
  137.4 92.7 all-gather.2
where the time goes:
time: 244 us
  waiting for transfers between devices  104 us (43%)
  blocking collectives  41.9 us (17%)
  matrix products  25.6 us (10%)
  starting transfers between devices  21.8 us (9%)
  other arithmetic  19.9 us (8%)
  between operations  16.2 us (7%)
  local copies, waits for them, and re-layouts  14.2 us (6%)
    all_to_all x1, waiting for transfers between devices, per_device(): lax.all_to_all(outgoing.reshape(slot_count, capacity, row_width), ('ep',...  91.9 us
    all_gather x1, blocking collectives, per_device(): lax.all_gather(flat_a.astype(jnp.bfloat16), 'ex', axis=0, tiled=True)  41.9 us
    dot_general x1, matrix products, expert_row_block(): jnp.dot(dsc_low, frozen_w.T, preferred_element_type=jnp.float32)  11.3 us
    scatter x1, other arithmetic, per_device(): jnp.zeros((slot_count * capacity, row_width), jnp.bfloat16).at[buffer_row]  9.96 us
    all_gather x1, waiting for transfers between devices, per_device(): lax.all_gather(flat_b.astype(jnp.bfloat16), 'ex', axis=0, tiled=True)  9.41 us
    all_to_all x1, starting transfers between devices, per_device(): lax.all_to_all(outgoing_gate.reshape(slot_count, capacity), ('ep', 'ex'),...  7.3 us
    all_to_all x1, starting transfers between devices, per_device(): lax.all_to_all(outgoing.reshape(slot_count, capacity, row_width), ('ep',...  5.96 us
    all_to_all x1, starting transfers between devices, per_device(): lax.all_to_all(gated_output.reshape(slot_count, capacity), ('ep', 'ex'),...  5.36 us
  transfers between devices with their start and end apart: 5, of which 3 were waited for; matrix products, arithmetic and copies ran while one was open for 17% of the time, Pallas kernels for 0%

commit v1 on v0

--- a/solution.py
+++ b/solution.py
@@ -10,6 +10,24 @@
 learn_rate = 0.01
 weight_decay = 0.01
 adam_step = 10
+
+
+def collect(array, axis, dim):
+    ways, here, step = (lax.axis_size(axis), lax.axis_index(axis), array.shape[dim])
+    dims = [n * ways if d == dim else n for d, n in enumerate(array.shape)]
+    full = lax.dynamic_update_slice_in_dim(
+        jnp.zeros(dims, array.dtype), array, here * step, axis=dim
+    )
+    going_up = going_down = array
+    for far in range(1, ways // 2 + 1):
+        going_up = lax.ppermute(going_up, axis, [(d, (d + 1) % ways) for d in range(ways)])
+        full = lax.dynamic_update_slice_in_dim(full, going_up, (here - far) % ways * step, axis=dim)
+        if 2 * far < ways:
+            going_down = lax.ppermute(going_down, axis, [(d, (d - 1) % ways) for d in range(ways)])
+            full = lax.dynamic_update_slice_in_dim(
+                full, going_down, (here + far) % ways * step, axis=dim
+            )
+    return full
 
 
 def expert_row_block(
@@ -184,7 +202,7 @@
     flat_a = down_factor_gradient.reshape(1, hidden * adapter_rank_width // 128, 128)
     flat_b = up_factor_gradient.reshape(1, adapter_rank_width, model_width)
     pieces = (
-        lax.all_gather(flat_a.astype(jnp.bfloat16), "ex", axis=0, tiled=True).astype(jnp.float32),
+        collect(flat_a.astype(jnp.bfloat16), "ex", 0).astype(jnp.float32),
         lax.all_gather(flat_b.astype(jnp.bfloat16), "ex", axis=0, tiled=True).astype(jnp.float32),
     )
     length = pieces[0].shape[0]

time: 244 us -> 244 us (level)
  blocking collectives: 41.9 us -> 0 us
  waiting for transfers between devices: 104 us -> 129 us
  starting transfers between devices: 21.8 us -> 38.4 us
    all_gather x1 -> x0, blocking collectives: 41.9 us -> none  [per_device(): lax.all_gather(flat_a.astype(jnp.bfloat16), 'ex', axis=0, tiled=True)]
    ppermute x0 -> x3, waiting for transfers between devices: none -> 25.3 us  [the longest x2 25.3 us: collect(): lax.ppermute(going_up, axis, [(d, (d + 1) % ways) for d in range(ways)])]
    ppermute x0 -> x3, starting transfers between devices: none -> 16.4 us  [the longest x2 14.4 us: collect(): lax.ppermute(going_up, axis, [(d, (d + 1) % ways) for d in range(ways)])]
  transfers between devices with their start and end apart: 5 -> 8, of which waited for: 3 -> 5; matrix products, arithmetic and copies ran while one was open for 17% -> 17% of each run, Pallas kernels for 0% -> 0%
where the time goes in v1:
time: 244 us
  waiting for transfers between devices  129 us (53%)
  starting transfers between devices  38.4 us (16%)
  matrix products  25.7 us (11%)
  other arithmetic  19.8 us (8%)
  between operations  16.3 us (7%)
  local copies, waits for them, and re-layouts  14.3 us (6%)
    all_to_all x1, waiting for transfers between devices, per_device(): lax.all_to_all(outgoing.reshape(slot_count, capacity, row_width), ('ep',...  91.9 us
    ppermute x2, waiting for transfers between devices, collect(): lax.ppermute(going_up, axis, [(d, (d + 1) % ways) for d in range(ways)])  25.3 us
    ppermute x2, starting transfers between devices, collect(): lax.ppermute(going_up, axis, [(d, (d + 1) % ways) for d in range(ways)])  14.4 us
    dot_general x1, matrix products, expert_row_block(): jnp.dot(dsc_low, frozen_w.T, preferred_element_type=jnp.float32)  11.3 us
    scatter x1, other arithmetic, per_device(): jnp.zeros((slot_count * capacity, row_width), jnp.bfloat16).at[buffer_row]  9.96 us
    all_gather x1, waiting for transfers between devices, per_device(): lax.all_gather(flat_b.astype(jnp.bfloat16), 'ex', axis=0, tiled=True)  9.31 us
    all_to_all x1, starting transfers between devices, per_device(): lax.all_to_all(outgoing_gate.reshape(slot_count, capacity), ('ep', 'ex'),...  7.3 us
    all_to_all x1, starting transfers between devices, per_device(): lax.all_to_all(outgoing.reshape(slot_count, capacity, row_width), ('ep',...  5.96 us
  transfers between devices with their start and end apart: 8, of which 5 were waited for; matrix products, arithmetic and copies ran while one was open for 17% of the time, Pallas kernels for 0%

profile of v1, /device:TPU:0, one launch (start us, length us, event | category | flops | bytes accessed | tf_op | source)
XLA Modules:
  0.0 243.8 jit_solution(8940300245096639061)
XLA Ops:
  7.2 0.8 copy.56
  8.3 0.8 fusion.49
  9.2 0.8 copy.57
  10.1 2.2 scatter_custom_fusion
  12.3 0.7 all_to_all.21
  13.0 7.3 %all-to-all-start = ((bf16[32,1,8]{2,1,0:T(2,128)(2,1)}), bf16[32,1,8]{2,1,0:T(2,128)(2,1)S(1)}, u32[]{:S(2)}, u32[]{:S(2)}) async-start(bf16[32,1,8]{2,1,0:T(2,128)(2,1)} %all_to_all.21), calls=%async_computation | async-start | bytes 32768 | tf_op jit(solution)/shard_map/all_to_all | solution.py:153
  20.3 3.3 %broadcast_in_dim.59 = bf16[32,8,7168]{2,1,0:T(8,128)(2,1)} broadcast(bf16[32,7168]{1,0:T(8,128)(2,1)} %param.14), dimensions={0,2} | broadcast | bytes 4128768 | tf_op jit(solution)/shard_map/broadcast_in_dim | solution.py:134
  23.6 10.0 %scatter_custom_fusion.1 = bf16[256,8192]{1,0:T(8,128)(2,1)} fusion(s32[256]{0:T(256)S(1)} %bitcast.56, bf16[32,8,1024]{2,1,0:T(8,128)(2,1)S(1)} %copy-done.3, bf16[]{:T(256)} %constant.119, bf16[32,8,7168]{2,1,0:T(8,128)(2,1)} %broadcast_in_dim.59, bf16[]{:T(256)} %constant.38.clone.1), kind=kCustom, calls=%fused_computation.15 | custom fusion | flops 8388608 | bytes 8388612 | tf_op jit(solution)/shard_map/scatter | solution.py:138
  33.6 6.0 %all-to-all-start.1 = ((bf16[32,8,8192]{2,1,0:T(8,128)(2,1)}), bf16[32,8,8192]{2,1,0:T(8,128)(2,1)}, u32[]{:S(2)}, u32[]{:S(2)}) async-start(bf16[32,8,8192]{2,1,0:T(8,128)(2,1)} %bitcast.49), calls=%async_computation.1 | async-start | bytes 8388608 | tf_op jit(solution)/shard_map/all_to_all | solution.py:146
  39.9 91.9 %all-to-all-done.1 = bf16[32,8,8192]{2,1,0:T(8,128)(2,1)} async-done(((bf16[32,8,8192]{2,1,0:T(8,128)(2,1)}), bf16[32,8,8192]{2,1,0:T(8,128)(2,1)}, u32[]{:S(2)}, u32[]{:S(2)}) %all-to-all-start.1) | async-done | bytes 4194336 | tf_op jit(solution)/shard_map/all_to_all | solution.py:146
  131.8 1.3 convolution_convert_fusion
  133.2 4.1 %fusion.2 = bf16[64,7168]{1,0:T(8,128)(2,1)} fusion(bf16[256,64]{0,1:T(8,128)(2,1)S(1)} %convolution_convert_fusion, f32[256]{0:T(256)S(1)} %reshape.282, bf16[256,8192]{1,0:T(8,128)(2,1)} %bitcast.7), kind=kOutput, calls=%fused_computation.9 | convolution fusion | flops 241303552 | bytes 4621312 | tf_op jit(solution)/shard_map/dot_general | solution.py:71
  139.9 3.3 %fusion.27 = f32[256]{0:T(256)S(1)} fusion(bf16[256,8192]{1,0:T(8,128)(2,1)} %bitcast.7, bf16[1,64,7168]{2,1,0:T(8,128)(2,1)S(1)} %copy-done, bf16[256,64]{0,1:T(8,128)(2,1)S(1)} %convolution_convert_fusion), kind=kOutput, calls=%fused_computation.41 | convolution fusion | flops 234929920 | bytes 4621312 | tf_op jit(solution)/shard_map/dot_general | solution.py:60
  143.2 11.3 %multiply_reduce_fusion.1 = (f32[256]{0:T(256)S(1)}, f32[256,1024]{1,0:T(8,128)S(1)}) fusion(bf16[256,8192]{1,0:T(8,128)(2,1)} %bitcast.7, bf16[1,1024,7168]{2,1,0:T(8,128)(2,1)} %param.20, f32[7168]{0:T(1024)S(1)} %bitcast.59), kind=kOutput, calls=%fused_computation.44 | convolution fusion | flops 3764387584 | bytes 19952640 | tf_op jit(solution)/shard_map/dot_general | solution.py:49
  154.5 0.7 convert_element_type.158
  155.2 5.3 %all-to-all-start.3 = ((bf16[32,1,8]{2,1,0:T(2,128)(2,1)}), bf16[32,1,8]{2,1,0:T(2,128)(2,1)S(1)}, u32[]{:S(2)}, u32[]{:S(2)}) async-start(bf16[32,1,8]{2,1,0:T(2,128)(2,1)} %convert_element_type.158), calls=%async_computation.3 | async-start | bytes 32768 | tf_op jit(solution)/shard_map/all_to_all | solution.py:184
  160.5 3.4 %convolution_convert_fusion.1 = bf16[256,64]{0,1:T(8,128)(2,1)S(1)} fusion(f32[256]{0:T(256)S(1)} %reshape.282, bf16[256,8192]{1,0:T(8,128)(2,1)} %bitcast.7, bf16[1,64,7168]{2,1,0:T(8,128)(2,1)S(1)} %copy-done), kind=kOutput, calls=%fused_computation.40 | convolution fusion | flops 240402432 | bytes 4621312 | tf_op jit(solution)/shard_map/dot_general | solution.py:46
  163.9 1.1 fusion.22
  165.0 2.8 %all-to-all-done.3 = bf16[32,1,8]{2,1,0:T(2,128)(2,1)S(1)} async-done(((bf16[32,1,8]{2,1,0:T(2,128)(2,1)}), bf16[32,1,8]{2,1,0:T(2,128)(2,1)S(1)}, u32[]{:S(2)}, u32[]{:S(2)}) %all-to-all-start.3) | async-done | bytes 544 | tf_op jit(solution)/shard_map/all_to_all | solution.py:184
  167.9 3.1 %all-to-all-start.2 = ((bf16[32,8,1024]{2,1,0:T(8,128)(2,1)}), bf16[32,8,1024]{2,1,0:T(8,128)(2,1)S(1)}, u32[]{:S(2)}, u32[]{:S(2)}) async-start(bf16[32,8,1024]{2,1,0:T(8,128)(2,1)} %fusion.22), calls=%async_computation.2 | async-start | bytes 1048576 | tf_op jit(solution)/shard_map/all_to_all | solution.py:177
  171.0 1.3 fusion.23
  172.6 1.8 collective-permute-start
  174.4 2.1 collective-permute-start.1
  176.7 1.9 gather_fusion.1
  179.3 19.3 %collective-permute-done = bf16[1,512,128]{2,1,0:T(8,128)(2,1)S(1)} collective-permute-done((bf16[1,512,128]{2,1,0:T(8,128)(2,1)S(1)}, bf16[1,512,128]{2,1,0:T(8,128)(2,1)S(1)}, u32[]{:S(2)}, u32[]{:S(2)}) %collective-permute-start) | collective-permute-done | bytes 131104 | tf_op jit(solution)/shard_map/ppermute | solution.py:23
  198.7 12.5 %collective-permute-start.2 = (bf16[1,512,128]{2,1,0:T(8,128)(2,1)S(1)}, bf16[1,512,128]{2,1,0:T(8,128)(2,1)S(1)}, u32[]{:S(2)}, u32[]{:S(2)}) collective-permute-start(bf16[1,512,128]{2,1,0:T(8,128)(2,1)S(1)} %collective-permute-done), channel_id=1, source_target_pairs={{0,1},{1,2},{2,3},{3,0},{4,5},{5,6},{6,7},{7,4},{8,9},{9,10},{10,1... | collective-permute-start | bytes 393224 | tf_op jit(solution)/shard_map/ppermute | solution.py:23
  211.3 6.0 %collective-permute-done.2 = bf16[1,512,128]{2,1,0:T(8,128)(2,1)S(1)} collective-permute-done((bf16[1,512,128]{2,1,0:T(8,128)(2,1)S(1)}, bf16[1,512,128]{2,1,0:T(8,128)(2,1)S(1)}, u32[]{:S(2)}, u32[]{:S(2)}) %collective-permute-start.2) | collective-permute-done | bytes 131104 | tf_op jit(solution)/shard_map/ppermute | solution.py:23
  217.8 1.0 fusion.45
  218.9 2.0 gather_fusion
  220.8 9.3 %all-gather.3.cloned.1.call-done = bf16[256,7168]{1,0:T(8,128)(2,1)} async-done(((bf16[64,7168]{1,0:T(8,128)(2,1)}), bf16[256,7168]{1,0:T(8,128)(2,1)}) %all-gather.3.cloned.1.call-update) | async-done | bytes 3670032 | tf_op jit(solution)/shard_map/all_gather | solution.py:206
  230.2 3.1 %fusion.5 = f32[64,7168]{1,0:T(8,128)S(1)} fusion(bf16[4,64,7168]{2,1,0:T(8,128)(2,1)} %bitcast.50, f32[4]{0:T(128)S(1)} %or_convert_fusion), kind=kLoop, calls=%fused_computation.13 | loop fusion | flops 5046272 | bytes 5505040 | tf_op jit(solution)/shard_map/reduce_sum | solution.py:214
  233.2 3.7 %fusion.33 = (bf16[1,64,7168]{2,1,0:T(8,128)(2,1)}, bf16[1,64,7168]{2,1,0:T(8,128)(2,1)}, bf16[1,64,7168]{2,1,0:T(8,128)(2,1)}) fusion(f32[64,7168]{1,0:T(8,128)S(1)} %fusion.5, bf16[1,64,7168]{2,1,0:T(8,128)(2,1)S(1)} %copy-done.1, bf16[1,64,7168]{2,1,0:T(8,128)(2,1)S(1)} %copy-done.2, bf16[1,64,7168]{2,1,0:T(8,128)(2,1)S(1)} %copy-done), kind=kLoop, calls=%fused_computation.45 | loop fusion | flops 9633792 | bytes 7340032 | tf_op jit(solution)/shard_map/convert_element_type | solution.py:91
  (49 shorter events, 3.5 us)
Async XLA Ops:
  7.2 16.5 %copy-start.3 = (bf16[32,8,1024]{2,1,0:T(8,128)(2,1)S(1)}, bf16[32,8,1024]{2,1,0:T(8,128)(2,1)}, u32[]{:S(2)}) copy-start(bf16[32,8,1024]{2,1,0:T(8,128)(2,1)} %param.16) | copy-start | bytes 1572868
  13.0 20.6 %all-to-all-start = ((bf16[32,1,8]{2,1,0:T(2,128)(2,1)}), bf16[32,1,8]{2,1,0:T(2,128)(2,1)S(1)}, u32[]{:S(2)}, u32[]{:S(2)}) async-start(bf16[32,1,8]{2,1,0:T(2,128)(2,1)} %all_to_all.21), calls=%async_computation | async-start | bytes 32768 | tf_op jit(solution)/shard_map/all_to_all | solution.py:153
  33.6 98.2 %copy-start.4 = (bf16[1,1024,64]{1,2,0:T(8,128)(2,1)S(1)}, bf16[1,1024,64]{1,2,0:T(8,128)(2,1)}, u32[]{:S(2)}) copy-start(bf16[1,1024,64]{1,2,0:T(8,128)(2,1)} %param.22) | copy-start | bytes 393220
  33.6 98.2 %all-to-all-start.1 = ((bf16[32,8,8192]{2,1,0:T(8,128)(2,1)}), bf16[32,8,8192]{2,1,0:T(8,128)(2,1)}, u32[]{:S(2)}, u32[]{:S(2)}) async-start(bf16[32,8,8192]{2,1,0:T(8,128)(2,1)} %bitcast.49), calls=%async_computation.1 | async-start | bytes 8388608 | tf_op jit(solution)/shard_map/all_to_all | solution.py:146
  39.6 190.6 %all-gather.3.cloned.1.call-start = ((), (), s32[]{:S(2)}) async-start(), calls=%async_computation.4 | async-start | bytes 4587520 | tf_op jit(solution)/shard_map/all_gather | solution.py:206
  133.1 4.1 %copy-start.8 = (s32[32]{0:T(128)S(1)}, s32[32]{0:T(128)}, u32[]{:S(2)}) copy-start(s32[32]{0:T(128)} %param.19) | copy-start | bytes 388
  133.1 6.7 %copy-start = (bf16[1,64,7168]{2,1,0:T(8,128)(2,1)S(1)}, bf16[1,64,7168]{2,1,0:T(8,128)(2,1)}, u32[]{:S(2)}) copy-start(bf16[1,64,7168]{2,1,0:T(8,128)(2,1)} %param.23) | copy-start | bytes 2752516
  137.2 6.0 %copy-start.7 = (f32[1,7168]{1,0:T(1,128)S(1)}, f32[1,7168]{1,0:T(1,128)}, u32[]{:S(2)}) copy-start(f32[1,7168]{1,0:T(1,128)} %param.21) | copy-start | bytes 86020
  155.2 12.7 %all-to-all-start.3 = ((bf16[32,1,8]{2,1,0:T(2,128)(2,1)}), bf16[32,1,8]{2,1,0:T(2,128)(2,1)S(1)}, u32[]{:S(2)}, u32[]{:S(2)}) async-start(bf16[32,1,8]{2,1,0:T(2,128)(2,1)} %convert_element_type.158), calls=%async_computation.3 | async-start | bytes 32768 | tf_op jit(solution)/shard_map/all_to_all | solution.py:184
  165.0 52.8 %copy-start.5 = (bf16[1,1024,64]{1,2,0:T(8,128)(2,1)S(1)}, bf16[1,1024,64]{1,2,0:T(8,128)(2,1)}, u32[]{:S(2)}) copy-start(bf16[1,1024,64]{1,2,0:T(8,128)(2,1)} %param.25) | copy-start | bytes 393220
  165.0 52.8 %copy-start.6 = (bf16[1,1024,64]{1,2,0:T(8,128)(2,1)S(1)}, bf16[1,1024,64]{1,2,0:T(8,128)(2,1)}, u32[]{:S(2)}) copy-start(bf16[1,1024,64]{1,2,0:T(8,128)(2,1)} %param.24) | copy-start | bytes 393220
  167.9 51.0 %all-to-all-start.2 = ((bf16[32,8,1024]{2,1,0:T(8,128)(2,1)}), bf16[32,8,1024]{2,1,0:T(8,128)(2,1)S(1)}, u32[]{:S(2)}, u32[]{:S(2)}) async-start(bf16[32,8,1024]{2,1,0:T(8,128)(2,1)} %fusion.22), calls=%async_computation.2 | async-start | bytes 1048576 | tf_op jit(solution)/shard_map/all_to_all | solution.py:177
  172.6 26.1 %collective-permute-start = (bf16[1,512,128]{2,1,0:T(8,128)(2,1)S(1)}, bf16[1,512,128]{2,1,0:T(8,128)(2,1)S(1)}, u32[]{:S(2)}, u32[]{:S(2)}) collective-permute-start(bf16[1,512,128]{2,1,0:T(8,128)(2,1)S(1)} %convert_element_type.141), channel_id=1, source_target_pairs={{0,1},{1,2},{2,3},{3,0},{4,5},{5,6},{6,7},{7,4},{8,9},{9,10},{10,1... | collective-permute-start | bytes 393224 | tf_op jit(solution)/shard_map/ppermute | solution.py:23
  174.4 36.8 %collective-permute-start.1 = (bf16[1,512,128]{2,1,0:T(8,128)(2,1)S(1)}, bf16[1,512,128]{2,1,0:T(8,128)(2,1)S(1)}, u32[]{:S(2)}, u32[]{:S(2)}) collective-permute-start(bf16[1,512,128]{2,1,0:T(8,128)(2,1)S(1)} %convert_element_type.141), channel_id=1, source_target_pairs={{0,3},{1,0},{2,1},{3,2},{4,7},{5,4},{6,5},{7,6},{8,11},{9,8},{10,9... | collective-permute-start | bytes 393224 | tf_op jit(solution)/shard_map/ppermute | solution.py:26
  198.7 18.6 %collective-permute-start.2 = (bf16[1,512,128]{2,1,0:T(8,128)(2,1)S(1)}, bf16[1,512,128]{2,1,0:T(8,128)(2,1)S(1)}, u32[]{:S(2)}, u32[]{:S(2)}) collective-permute-start(bf16[1,512,128]{2,1,0:T(8,128)(2,1)S(1)} %collective-permute-done), channel_id=1, source_target_pairs={{0,1},{1,2},{2,3},{3,0},{4,5},{5,6},{6,7},{7,4},{8,9},{9,10},{10,1... | collective-permute-start | bytes 393224 | tf_op jit(solution)/shard_map/ppermute | solution.py:23
  220.8 12.4 %copy-start.1 = (bf16[1,64,7168]{2,1,0:T(8,128)(2,1)S(1)}, bf16[1,64,7168]{2,1,0:T(8,128)(2,1)}, u32[]{:S(2)}) copy-start(bf16[1,64,7168]{2,1,0:T(8,128)(2,1)} %param.27) | copy-start | bytes 2752516
  220.8 12.4 %copy-start.2 = (bf16[1,64,7168]{2,1,0:T(8,128)(2,1)S(1)}, bf16[1,64,7168]{2,1,0:T(8,128)(2,1)}, u32[]{:S(2)}) copy-start(bf16[1,64,7168]{2,1,0:T(8,128)(2,1)} %param.26) | copy-start | bytes 2752516
Sparse Core Ops, SparseCore 0:
  137.4 92.7 all-gather.2
